TPU v7x, 256 devices: a whole 4x4x8 slice. The times are simulated.
256 devices in a mesh: ens: 4 (over y), space: 64 (over z, x, core).
Axes of the slice: x: 4, y: 4, z: 8, core: 2. Of those that a mesh axis runs over, the one named last changes fastest.
Arguments:
- latents: bfloat16 [8, 16384, 1024], P('ens', 'space'), may hold values from -6 to 6
- edge_index: int32 [32768, 4], P('space'), may hold values from 0 to 767, as said below
- edge_weight: float32 [32768, 4], P('space'), may hold values from 0.1 to 1
- truth: float32 [100, 32768], P(None, 'space'), may hold values from -6 to 6
- w_hidden: bfloat16 [1024, 1024], replicated, may hold values from -0.1875 to 0.1875
- output_weight: bfloat16 [1024, 100], replicated, may hold values from -0.1875 to 0.1875
Outputs:
- grad_latents: float32 [8, 16384, 1024], P('ens', 'space')
- grad_hidden: float32 [1024, 1024], P('space')
- grad_out: float32 [1024, 100], P('space')
Inputs may be any that keep to these rules, and one draw needn't show every extreme that they name: edge_index of a grid point holds 4 distinct values, indexing the nodes of the bands below, own and above; the first band never points below and the last never above.
All inputs are finite; a program needn't handle non-finite values.
Results may differ from a plain program's by a relative error of at most 0.012.
The roundings to bfloat16 on the way count: a program that leaves them out, or rounds other values in their place, can miss the bound.
Values may be sent and summed in bfloat16 or wider, within the bound.
A program may use at most 64 MiB of HBM per device.

v0:
```python
import math

import jax
import jax.numpy as jnp
from jax import lax
from jax.sharding import PartitionSpec as P

smoothing = 0.05


def extended(cells, sides, width):
    for axis, dim in sides:
        count = lax.axis_size(axis)
        ends = count - 1
        head = lax.slice_in_dim(cells, 0, width, axis=dim)
        tail = lax.slice_in_dim(cells, cells.shape[dim] - width, cells.shape[dim], axis=dim)
        cells = jnp.concatenate(
            [
                lax.ppermute(tail, axis, [(i, (i + 1) % count) for i in range(ends)]),
                cells,
                lax.ppermute(head, axis, [((i + 1) % count, i) for i in range(ends)]),
            ],
            axis=dim,
        )
    return cells


def from_behind(value, axis, steps):
    count = lax.axis_size(axis)
    first, last = (max(0, -steps), min(count, count - steps))
    return lax.ppermute(value, axis, [(source, source + steps) for source in range(first, last)])


def silu_slope(preact):
    logistic = jax.nn.sigmoid(preact)
    return logistic * (1.0 + preact * (1.0 - logistic))


def pairwise_total(mine, others):
    pairwise_distance = mine[:, None] - others[None, :]
    return jnp.sum(
        pairwise_distance / jnp.sqrt(pairwise_distance * pairwise_distance + smoothing * smoothing),
        axis=1,
    )


def shards(latents, edge_index, edge_weight, truth, w_hidden, output_weight):
    mem_dev, nodes_dev, hidden_width = latents.shape
    grid_dev = truth.shape[1]
    members = mem_dev * lax.axis_size("ens")
    grid_cells = grid_dev * lax.axis_size("space")
    loss_scale = 1.0 / math.sqrt(grid_cells * members)
    window = extended(latents, (("space", 1),), nodes_dev)
    rounded = lax.optimization_barrier(edge_weight.astype(jnp.bfloat16)).astype(jnp.float32)
    column = lax.broadcasted_iota(jnp.int32, (1, 1, 3 * nodes_dev), 2)
    adjacency = jnp.sum(
        jnp.where(edge_index[:, :, None] == column, rounded[:, :, None], 0.0), axis=1
    ).astype(jnp.bfloat16)
    aggregate = jnp.einsum(
        "gn,mnh->mgh", adjacency, window, preferred_element_type=jnp.float32
    ).astype(jnp.bfloat16)
    preact = jnp.einsum("mgh,hk->mgk", aggregate, w_hidden, preferred_element_type=jnp.float32)
    activation_values = jax.nn.silu(preact).astype(jnp.bfloat16)
    member_prediction = jnp.einsum(
        "pak,kc->pca", activation_values, output_weight, preferred_element_type=jnp.float32
    )
    error_residual = member_prediction - truth[None]
    distance = jnp.sqrt(error_residual * error_residual + smoothing * smoothing)
    all_members_view = lax.all_gather(member_prediction, "ens", axis=0, tiled=True)
    ensemble_spread = pairwise_total(member_prediction, all_members_view)
    dforecast = (
        loss_scale
        * (error_residual / (members * distance) - ensemble_spread / (members * (members - 1)))
    ).astype(jnp.bfloat16)
    out_part = jnp.einsum(
        "mgh,mvg->hv", activation_values, dforecast, preferred_element_type=jnp.float32
    )
    dactivated = jnp.einsum(
        "mvg,hv->mgh", dforecast, output_weight, preferred_element_type=jnp.float32
    )
    dpreact = (dactivated * silu_slope(preact)).astype(jnp.bfloat16)
    hidden_part = jnp.einsum("mgh,mgk->hk", aggregate, dpreact, preferred_element_type=jnp.float32)
    daggregate = jnp.einsum(
        "mgk,hk->mgh", dpreact, w_hidden, preferred_element_type=jnp.float32
    ).astype(jnp.bfloat16)
    grad_window = jnp.einsum(
        "gn,mgh->mnh", adjacency, daggregate, preferred_element_type=jnp.float32
    )
    lower_part = grad_window[:, :nodes_dev]
    own_part = grad_window[:, nodes_dev : 2 * nodes_dev]
    upper_part = grad_window[:, 2 * nodes_dev :]
    from_above = from_behind(lower_part, "space", -1)
    from_below = from_behind(upper_part.astype(jnp.bfloat16), "space", 1).astype(upper_part.dtype)
    grad_latents = own_part + from_above + from_below
    summed = lax.psum((hidden_part, out_part), "ens")
    grad_hidden, grad_out = (
        lax.psum_scatter(summed[0], "space", scatter_dimension=0, tiled=True),
        lax.psum_scatter(summed[1], "space", scatter_dimension=0, tiled=True),
    )
    return (grad_latents, grad_hidden, grad_out)


def solution(mesh):
    placed = (
        P("ens", "space", None),
        P("space", None),
        P("space", None),
        P(None, "space"),
        P(),
        P(),
    )
    return jax.shard_map(
        shards,
        mesh=mesh,
        in_specs=placed,
        out_specs=(P("ens", "space", None), P("space", None), P("space", None)),
        check_vma=False,
    )
```

profile of v0, /device:TPU:2, one launch (start us, length us, event | category | flops | bytes accessed | tf_op | source)
XLA Modules:
  0.0 466.8 jit_solution(12787110133032285526)
XLA Ops:
  7.2 1.6 copy.25
  8.8 1.9 collective-permute-start.1
  10.8 2.4 collective-permute-start
  13.9 1.7 select_reduce_fusion
  15.6 7.5 %collective-permute-done.1 = bf16[2,256,1024]{1,2,0:T(8,128)(2,1)S(1)} collective-permute-done((bf16[2,256,1024]{1,2,0:T(8,128)(2,1)S(1)}, bf16[2,256,1024]{1,2,0:T(8,128)(2,1)S(1)}, u32[]{:S(2)}, u32[]{:S(2)}) %collective-permute-start.1) | collective-permute-done | bytes 1048608 | tf_op jit(solution)/shard_map/ppermute | solution.py:21
  23.1 4.5 collective-permute-done
  27.5 1.8 fusion.17
  29.4 4.8 %multiply_convert_fusion.1 = (bf16[2,512,1024]{2,1,0:T(8,128)(2,1)S(1)}, f32[2,512,1024]{2,1,0:T(8,128)}) fusion(bf16[1024,1024]{1,0:T(8,128)(2,1)S(1)} %copy-done, bf16[2,1024,512]{2,1,0:T(8,128)(2,1)S(1)} %fusion.17), kind=kOutput, calls=%fused_computation.5 | convolution fusion | flops 2152726528 | bytes 10485760 | tf_op jit(solution)/shard_map/mgh,hk->mgk/dot_general | solution.py:62
  35.6 1.6 convolution_bitcast_fusion.3
  37.2 35.2 %all-gather.2.cloned.1.call-done = f32[8,100,512]{2,1,0:T(8,128)} async-done(((f32[2,100,512]{2,1,0:T(8,128)}), f32[8,100,512]{2,1,0:T(8,128)}) %all-gather.2.cloned.1.call-update) | async-done | bytes 1638416 | tf_op jit(solution)/shard_map/all_gather | solution.py:69
  72.4 2.6 copy.29
  78.2 5.2 %multiply_convert_fusion = bf16[2,512,1024]{2,1,0:T(8,128)(2,1)} fusion(f32[2,512,1024]{2,1,0:T(8,128)} %get-tuple-element.13, bf16[2,100,512]{2,1,0:T(8,128)(2,1)S(1)} %multiply_convert_fusion.2, bf16[1024,100]{0,1:T(8,128)(2,1)S(1)} %copy-done.7), kind=kOutput, calls=%fused_computation.4 | convolution fusion | flops 219152384 | bytes 6701056 | tf_op jit(solution)/shard_map/mvg,hv->mgh/dot_general | solution.py:78
  83.7 6.6 %convolution_bitcast_fusion.1 = f32[1024,1024]{1,0:T(8,128)} fusion(bf16[2,512,1024]{2,1,0:T(8,128)(2,1)} %multiply_convert_fusion, bf16[2,1024,512]{2,1,0:T(8,128)(2,1)} %copy-done.9), kind=kOutput, calls=%fused_computation.17 | convolution fusion | flops 2147483648 | bytes 8388608 | tf_op jit(solution)/shard_map/mgh,mgk->hk/dot_general | solution.py:82
  91.4 8.3 %convolution_bitcast_fusion = f32[2,768,1024]{1,2,0:T(8,128)} fusion(bf16[2,512,1024]{2,1,0:T(8,128)(2,1)} %multiply_convert_fusion, bf16[1024,1024]{1,0:T(8,128)(2,1)S(1)} %copy-done, bf16[512,768]{1,0:T(8,128)(2,1)S(1)} %copy-done.5), kind=kOutput, calls=%fused_computation.16 | convolution fusion | flops 3759144960 | bytes 11272192 | tf_op jit(solution)/shard_map/gn,mgh->mnh/dot_general | solution.py:86
  99.6 3.1 slice.14
  102.7 1.9 collective-permute-start.2
  104.6 2.7 slice.20
  107.4 2.4 collective-permute-start.3
  111.0 155.7 %all-reduce.6.cloned.1.call-done = f32[1024,100]{1,0:T(8,128)} async-done(((f32[1024,100]{1,0:T(8,128)}), f32[1024,100]{1,0:T(8,128)}) %all-reduce.6.cloned.1.call-update) | async-done | bytes 409616
  267.4 11.1 %psum.17 = f32[16,100]{1,0:T(8,128)} all-reduce(f32[16,100]{1,0:T(8,128)S(1)} %constant_dynamic-slice_fusion), channel_id=1, replica_groups=mesh['ens'=4,'space'=64] {'ens'}, use_global_device_ids=true, to_apply=%region_4.5 | all-reduce | flops 1600 | bytes 12800 | tf_op jit(solution)/shard_map/psum | solution.py:95
  278.5 132.8 %reduce-scatter.2.cloned.1.call-done = f32[16,1024]{1,0:T(8,128)} async-done(((f32[1024,1024]{1,0:T(8,128)}), f32[16,1024]{1,0:T(8,128)}) %reduce-scatter.2.cloned.1.call-update) | async-done | bytes 65552 | tf_op jit(solution)/shard_map/reduce_scatter | solution.py:97
  411.4 3.9 fusion.9
  415.3 2.9 copy.32
  418.2 40.6 %all-reduce.4.cloned.1.call-done = f32[16,1024]{1,0:T(8,128)} async-done(((f32[16,1024]{1,0:T(8,128)}), f32[16,1024]{1,0:T(8,128)}) %all-reduce.4.cloned.1.call-update) | async-done | bytes 65552 | tf_op jit(solution)/shard_map/psum | solution.py:95
  (38 shorter events, 9.5 us)
Async XLA Ops:
  7.2 22.2 %copy-start = (bf16[1024,1024]{1,0:T(8,128)(2,1)S(1)}, bf16[1024,1024]{1,0:T(8,128)(2,1)}, u32[]{:S(2)}) copy-start(bf16[1024,1024]{1,0:T(8,128)(2,1)} %param.10) | copy-start | bytes 6291460
  7.2 65.3 %all-gather.2.cloned.1.call-start = ((), (), s32[]{:S(2)}) async-start(), calls=%async_computation.1 | async-start | bytes 2129920 | tf_op jit(solution)/shard_map/all_gather | solution.py:69
  8.8 14.2 %collective-permute-start.1 = (bf16[2,256,1024]{1,2,0:T(8,128)(2,1)S(1)}, bf16[2,256,1024]{1,2,0:T(8,128)(2,1)S(1)}, u32[]{:S(2)}, u32[]{:S(2)}) collective-permute-start(bf16[2,256,1024]{1,2,0:T(8,128)(2,1)S(1)} %copy.25), channel_id=1, source_target_pairs={{1,0},{2,1},{3,2},{4,3},{5,4},{6,5},{7,6},{8,7},{9,8},{10,9},{11,1... | collective-permute-start | bytes 3145736 | tf_op jit(solution)/shard_map/ppermute | solution.py:21
  10.8 16.8 %collective-permute-start = (bf16[2,256,1024]{1,2,0:T(8,128)(2,1)S(1)}, bf16[2,256,1024]{1,2,0:T(8,128)(2,1)S(1)}, u32[]{:S(2)}, u32[]{:S(2)}) collective-permute-start(bf16[2,256,1024]{1,2,0:T(8,128)(2,1)S(1)} %copy.25), channel_id=1, source_target_pairs={{0,1},{1,2},{2,3},{3,4},{4,5},{5,6},{6,7},{7,8},{8,9},{9,10},{10,1... | collective-permute-start | bytes 3145736 | tf_op jit(solution)/shard_map/ppermute | solution.py:19
  15.6 13.8 %copy-start.4 = (bf16[512,768]{1,0:T(8,128)(2,1)}, bf16[512,768]{1,0:T(8,128)(2,1)S(1)}, u32[]{:S(2)}) copy-start(bf16[512,768]{1,0:T(8,128)(2,1)S(1)} %select_reduce_fusion) | copy-start | bytes 2359300
  29.4 4.8 %copy-start.9 = (bf16[2,1024,512]{2,1,0:T(8,128)(2,1)}, bf16[2,1024,512]{2,1,0:T(8,128)(2,1)S(1)}, u32[]{:S(2)}) copy-start(bf16[2,1024,512]{2,1,0:T(8,128)(2,1)S(1)} %fusion.17) | copy-start | bytes 6291460
  29.4 6.2 %copy-start.7 = (bf16[1024,100]{0,1:T(8,128)(2,1)S(1)}, bf16[1024,100]{0,1:T(8,128)(2,1)}, u32[]{:S(2)}) copy-start(bf16[1024,100]{0,1:T(8,128)(2,1)} %param.11) | copy-start | bytes 614404
  34.2 1.3 copy-start.1
  37.2 37.8 %copy-start.3 = (f32[2,100,512]{2,1,0:T(8,128)S(1)}, f32[2,100,512]{2,1,0:T(8,128)}, u32[]{:S(2)}) copy-start(f32[2,100,512]{2,1,0:T(8,128)} %convolution_bitcast_fusion.3) | copy-start | bytes 1228804
  37.2 39.2 %copy-start.6 = (f32[100,512]{1,0:T(8,128)S(1)}, f32[100,512]{1,0:T(8,128)}, u32[]{:S(2)}) copy-start(f32[100,512]{1,0:T(8,128)} %param.9) | copy-start | bytes 614404
  37.2 229.5 %all-reduce.6.cloned.1.call-start = ((), (), s32[]{:S(2)}) async-start(), calls=%async_computation.4 | async-start | bytes 1048576
  72.4 4.2 copy-start.2
  83.4 327.9 %reduce-scatter.2.cloned.1.call-start = ((), (), s32[]{:S(2)}) async-start(), calls=%async_computation.2 | async-start | bytes 4259840 | tf_op jit(solution)/shard_map/reduce_scatter | solution.py:97
  90.2 1.1 copy-start.5
  90.3 368.5 %all-reduce.4.cloned.1.call-start = ((), (), s32[]{:S(2)}) async-start(), calls=%async_computation.3 | async-start | bytes 131072 | tf_op jit(solution)/shard_map/psum | solution.py:95
  99.6 10.1 %copy-start.8 = (u32[256]{0:T(256)S(1)}, u32[256]{0:T(256)}, u32[]{:S(2)}) copy-start(u32[256]{0:T(256)} %constant.19) | copy-start | bytes 3076
  102.7 308.6 %collective-permute-start.2 = (f32[2,256,1024]{1,2,0:T(8,128)}, f32[2,256,1024]{1,2,0:T(8,128)}, u32[]{:S(2)}, u32[]{:S(2)}) collective-permute-start(f32[2,256,1024]{1,2,0:T(8,128)} %slice.14), channel_id=1, source_target_pairs={{1,0},{2,1},{3,2},{4,3},{5,4},{6,5},{7,6},{8,7},{9,8},{10,9},{11,1... | collective-permute-start | bytes 6291464 | tf_op jit(solution)/shard_map/ppermute | solution.py:31
  107.4 304.0 %collective-permute-start.3 = (bf16[2,256,1024]{1,2,0:T(8,128)(2,1)}, bf16[2,256,1024]{1,2,0:T(8,128)(2,1)S(1)}, u32[]{:S(2)}, u32[]{:S(2)}) collective-permute-start(bf16[2,256,1024]{1,2,0:T(8,128)(2,1)} %slice.20), channel_id=1, source_target_pairs={{0,1},{1,2},{2,3},{3,4},{4,5},{5,6},{6,7},{7,8},{8,9},{9,10},{10,1... | collective-permute-start | bytes 3145736 | tf_op jit(solution)/shard_map/ppermute | solution.py:31
Sparse Core Ops, SparseCore 0:
  37.3 35.0 all-gather.1
  83.6 183.0 all-reduce.5
  270.8 140.4 reduce-scatter.1
  413.6 45.1 all-reduce.3
where the time goes:
time: 467 us
  waiting for transfers between devices  376 us (81%)
  matrix products  29.8 us (6%)
  local copies, waits for them, and re-layouts  18 us (4%)
  between operations  14.6 us (3%)
  blocking collectives  11.1 us (2%)
  starting transfers between devices  8.97 us (2%)
  other arithmetic  7.91 us (2%)
    unnamed x5, waiting for transfers between devices  156 us
    reduce_scatter x1, waiting for transfers between devices, shards(): lax.psum_scatter(summed[0], 'space', scatter_dimension=0, tiled=True)  133 us
    psum x1, waiting for transfers between devices, shards(): summed = lax.psum((hidden_part, out_part), 'ens')  40.6 us
    all_gather x1, waiting for transfers between devices, shards(): lax.all_gather(member_prediction, 'ens', axis=0, tiled=True)  35.2 us
    psum x1, blocking collectives, shards(): summed = lax.psum((hidden_part, out_part), 'ens')  11.1 us
    unnamed x25, local copies, waits for them, and re-layouts  9.67 us
  transfers between devices with their start and end apart: 8, of which 6 were waited for; matrix products, arithmetic and copies ran while one was open for 7% of the time, Pallas kernels for 0%

commit v1 on v0

v1 whole, which is shorter than its diff:
```python
import functools
import math

import jax
import jax.numpy as jnp
from jax import lax
from jax.experimental import pallas as pl
from jax.experimental.pallas import tpu as pltpu
from jax.sharding import PartitionSpec as P

MESH = pl.DeviceIdType.MESH
f32 = jnp.float32
bf16 = jnp.bfloat16
smoothing = 0.05

H = 1024
V = 100
VP = 128
NB = 256
G = 512
ENS = 4
NZ, NX = 8, 4
SPACE = NZ * NX * 2
QG = G // ENS
FC = 2
FW = H // FC
GC = 4
GW = H // GC
NJ = 2
ZJ = NZ // NJ


def mm(a, b):
    return jnp.dot(a, b, preferred_element_type=f32)


def cols(i, width):
    return pl.ds(pl.multiple_of(i * width, width), width)


def kernel(
    scale,
    lat, ei, ew, truth, w, wot,
    gl, gh, go,
    xw, at, a, wv, wt, wotr, wotv, wov, eiv, ewv, trr, trv, trt,
    aggc, aggt, pre, act, fcs, fcr, dfs, dfr, dfrt, dpre, daggc,
    low, up, rlow, rup, own,
    ghk, ghs, ghr, yk, ys, yr, xk, xs, xr, zr, ghv,
    gok, gos, gor, gzk, gzs, gzr, gxs, gxr, gyv, gyr,
    ld, fs, fr, es, er, bs, br, hs, hr, cs, cr, ysm, yrm, xsm, xrm, zsm, zrm, gsm, grm,
    gzsm, gzrm, gxsm, gxrm, gysm, gyrm, outsm,
):
    e = lax.axis_index("ens")
    s = lax.axis_index("space")
    z = s // 8
    x = (s // 2) % NX
    core = s % 2
    right = (e, (s + 1) % SPACE)
    left = (e, (s + SPACE - 1) % SPACE)
    mate = (e, z * 8 + x * 2 + (1 - core))
    ypeer = [((e + k) % ENS, s) for k in range(1, ENS)]
    xpeer = [(e, z * 8 + ((x + k) % NX) * 2 + core) for k in range(1, NX)]
    zpeer = [(e, ((z + k) % NZ) * 8 + x * 2 + core) for k in range(1, NZ)]

    def remote(src, dst, ssem, rsem, to):
        cp = pltpu.make_async_remote_copy(
            src_ref=src, dst_ref=dst, send_sem=ssem, recv_sem=rsem, device_id=to, device_id_type=MESH
        )
        sends.append(cp)
        return cp

    sends = []
    barrier = pltpu.get_barrier_semaphore()
    everyone = [left, right, mate] + ypeer + xpeer + zpeer
    for to in everyone:
        pl.semaphore_signal(barrier, inc=1, device_id=to, device_id_type=MESH)

    loads = [
        pltpu.make_async_copy(ei, eiv, ld.at[0]),
        pltpu.make_async_copy(ew, ewv, ld.at[1]),
        pltpu.make_async_copy(lat, xw.at[:, pl.ds(NB, NB)], ld.at[2]),
        pltpu.make_async_copy(w, wv, ld.at[3]),
        pltpu.make_async_copy(wot, wotr, ld.at[4]),
        pltpu.make_async_copy(truth.at[:, cols(e, QG)], trr, ld.at[5]),
    ]
    for cp in loads:
        cp.start()
    pl.semaphore_wait(barrier, len(everyone))

    halo = {}
    for m in range(2):
        for c in range(FC):
            i = m * FC + c
            part = lat.at[m, :, pl.ds(c * FW, FW)]
            up_cp = remote(part, xw.at[m, pl.ds(0, NB), pl.ds(c * FW, FW)], fs.at[0, i], fr.at[0, i], right)
            dn_cp = remote(part, xw.at[m, pl.ds(2 * NB, NB), pl.ds(c * FW, FW)], fs.at[1, i], fr.at[1, i], left)
            up_cp.start()
            dn_cp.start()
            halo[m, c] = (up_cp, dn_cp)

    loads[0].wait()
    loads[1].wait()
    wr = ewv[...].astype(bf16).astype(f32)

    @pl.loop(0, 3 * NB // 128)
    def _(b):
        row = lax.broadcasted_iota(jnp.int32, (128, G), 0) + b * 128
        t = jnp.zeros((128, G), f32)
        for k in range(4):
            t = jnp.where(row == eiv[pl.ds(k, 1), :], wr[k : k + 1, :], t)
        at[cols(b, 128), :] = t.astype(bf16)
        a[:, cols(b, 128)] = t.T.astype(bf16)

    loads[2].wait()
    loads[3].wait()

    @pl.loop(0, H // 128)
    def _(b):
        wt[:, cols(b, 128)] = wv[cols(b, 128), :].T

    loads[4].wait()
    loads[5].wait()
    wotv[...] = jnp.concatenate([wotr[...], jnp.zeros((VP - V, H), bf16)], axis=0)
    trv[...] = jnp.concatenate([trr[...], jnp.zeros((VP - V, QG), f32)], axis=0)
    wov[...] = wotv[...].T
    trt[...] = trv[...].T

    for m in range(2):
        for c in range(FC):
            for cp in halo[m, c]:
                cp.wait_recv()

            @pl.loop(0, FW // 256)
            def _(t):
                src = pl.ds(pl.multiple_of(c * FW + t * 256, 256), 256)
                part = mm(a[...], xw[m, :, src]).astype(bf16)
                aggc[:, cols(t, 256)] = part
                aggt[src, pl.ds(m * G, G)] = part.T

            @pl.loop(0, H // 256)
            def _(t):
                v = mm(aggc[...], wv[pl.ds(c * FW, FW), cols(t, 256)])
                if c > 0:
                    v = v + pre[m, :, cols(t, 256)]
                pre[m, :, cols(t, 256)] = v

        for k in range(ENS):
            r = (e + 1 + k) % ENS
            rows = cols(r, QG)

            @pl.loop(0, H // 256)
            def _(t):
                v = pre[m, rows, cols(t, 256)]
                sg = jax.nn.sigmoid(v)
                act[pl.ds(pl.multiple_of(m * G + r * QG, QG), QG), cols(t, 256)] = (v * sg).astype(bf16)
                pre[m, rows, cols(t, 256)] = sg * (1.0 + v * (1.0 - sg))

            fc = mm(act[pl.ds(pl.multiple_of(m * G + r * QG, QG), QG), :], wov[...])
            if k < ENS - 1:
                fcs[k, m] = fc
                remote(fcs.at[k, m], fcr.at[k, m], es.at[k, m], er.at[k, m], ypeer[k]).start()
            else:
                fcr[k, m] = fc

    for m in range(2):
        for k in range(ENS - 1):
            pltpu.make_async_remote_copy(
                src_ref=fcs.at[k, m], dst_ref=fcr.at[k, m], send_sem=es.at[k, m], recv_sem=er.at[k, m],
                device_id=ypeer[k], device_id_type=MESH,
            ).wait_recv()

    members = 2 * ENS

    @pl.loop(0, QG // 16)
    def _(b):
        rows = cols(b, 16)
        f = [fcr[i // 2, i % 2, rows, :] for i in range(members)]
        tr = trt[rows, :]
        total = [jnp.zeros((16, VP), f32) for _ in range(members)]
        for i in range(members):
            for j in range(i + 1, members):
                d = f[i] - f[j]
                q = d * lax.rsqrt(d * d + smoothing * smoothing)
                total[i] = total[i] + q
                total[j] = total[j] - q
        for i in range(members):
            d = f[i] - tr
            q = d * lax.rsqrt(d * d + smoothing * smoothing)
            dfs[i // 2, i % 2, rows, :] = (
                scale * (q * (1.0 / members) - total[i] * (1.0 / (members * (members - 1))))
            ).astype(bf16)

    for k in range(ENS - 1):
        back = ((e + ENS - 1 - k) % ENS, s)
        remote(dfs.at[k], dfr.at[:, cols(e, QG)], bs.at[k], br.at[k], back).start()
    dfr[:, cols(e, QG), :] = dfs[ENS - 1]
    for k in range(ENS - 1):
        src = (e + 1 + k) % ENS
        pltpu.make_async_remote_copy(
            src_ref=dfs.at[k], dst_ref=dfr.at[:, cols(src, QG)], send_sem=bs.at[k], recv_sem=br.at[k],
            device_id=((e + ENS - 1 - k) % ENS, s), device_id_type=MESH,
        ).wait_recv()

    def dpreact(m):
        @pl.loop(0, H // 256)
        def _(t):
            v = mm(dfr[m], wotv[:, cols(t, 256)])
            dpre[pl.ds(m * G, G), cols(t, 256)] = (v * pre[m, :, cols(t, 256)]).astype(bf16)

    grads = {}

    def node_grads(m, c):
        @pl.loop(0, GW // 256)
        def _(t):
            src = pl.ds(pl.multiple_of(c * GW + t * 256, 256), 256)
            daggc[...] = mm(dpre[pl.ds(m * G, G), :], wt[:, src]).astype(bf16)
            low[m, :, src] = mm(at[pl.ds(0, NB), :], daggc[...]).astype(bf16)
            up[m, :, src] = mm(at[pl.ds(2 * NB, NB), :], daggc[...]).astype(bf16)
            own[m, :, src] = mm(at[pl.ds(NB, NB), :], daggc[...])

        i = m * GC + c
        part = pl.ds(c * GW, GW)
        one = remote(low.at[m, :, part], rlow.at[m, :, part], hs.at[0, i], hr.at[0, i], left)
        two = remote(up.at[m, :, part], rup.at[m, :, part], hs.at[1, i], hr.at[1, i], right)
        one.start()
        two.start()
        grads[m, c] = (one, two)

    dpreact(0)
    for c in range(GC):
        node_grads(0, c)
    dpreact(1)

    for m in range(2):
        dfrt[:, pl.ds(m * G, G)] = dfr[m].T

    @pl.loop(0, H // 256)
    def _(t):
        v = mm(dfrt[...], act[:, cols(t, 256)]).T
        v = v.reshape(256 // 32, 2, 16, VP)
        mine = jnp.where(core == 0, v[:, 0], v[:, 1])
        other = jnp.where(core == 0, v[:, 1], v[:, 0])
        gok[cols(t, 8)] = mine
        gos[cols(t, 8)] = other.astype(bf16)

    gcp = remote(gos, gor, gsm.at[0], grm.at[0], mate)
    gcp.start()

    RJ = H // NJ
    gcore = []
    for j in range(NJ):
        @pl.loop(0, (RJ // 256) * (H // 256))
        def _(t):
            rb = t // (H // 256)
            cb = t % (H // 256)
            v = mm(aggt[pl.ds(pl.multiple_of(j * RJ + rb * 256, 256), 256), :], dpre[:, cols(cb, 256)])
            v = v.reshape(256 // 32, 2, 16, 256)
            groups = pl.ds(j * (RJ // 32) + rb * 8, 8)
            ghk[groups, :, cols(cb, 256)] = jnp.where(core == 0, v[:, 0], v[:, 1])
            ghs[groups, :, cols(cb, 256)] = jnp.where(core == 0, v[:, 1], v[:, 0]).astype(bf16)

        half = pl.ds(j * (RJ // 32), RJ // 32)
        cp = remote(ghs.at[half], ghr.at[half], cs.at[j], cr.at[j], mate)
        cp.start()
        gcore.append(cp)

    gcp.wait_recv()
    gzs[...] = (gok[...] + gor[...].astype(f32)).astype(bf16)
    gz = []
    for k in range(1, NZ):
        cp = remote(gzs.at[cols((z + k) % NZ, NX)], gzr.at[k - 1], gzsm.at[k - 1], gzrm.at[k - 1], zpeer[k - 1])
        cp.start()
        gz.append(cp)
    gzk[...] = gok[cols(z, NX)] + gor[cols(z, NX)].astype(f32)

    ycp = []
    QC = H // ENS
    for j in range(NJ):
        gcore[j].wait_recv()
        NG = RJ // 32

        @pl.loop(0, NG // 4)
        def _(t):
            groups = pl.ds(j * NG + t * 4, 4)
            v = ghk[groups] + ghr[groups].astype(f32)
            ghk[groups] = v
            ys[groups] = v.astype(bf16)

        half = pl.ds(j * NG, NG)
        for k in range(1, ENS):
            cp = remote(
                ys.at[half, :, cols((e + k) % ENS, QC)], yr.at[k - 1, half], ysm.at[k - 1, j], yrm.at[k - 1, j],
                ypeer[k - 1],
            )
            cp.start()
            ycp.append(cp)

    for c in range(GC):
        node_grads(1, c)

    for cp in gz:
        cp.wait_recv()
    v = gzk[...]
    for k in range(NZ - 1):
        v = v + gzr[k].astype(f32)
    gzk[...] = v
    gxs[...] = v.astype(bf16)
    gx = []
    for k in range(1, NX):
        cp = remote(gxs.at[(x + k) % NX], gxr.at[k - 1], gxsm.at[k - 1], gxrm.at[k - 1], xpeer[k - 1])
        cp.start()
        gx.append(cp)

    outs = []
    for m in range(2):
        for c in range(GC):
            for cp in grads[m, c]:
                cp.wait_recv()
            part = pl.ds(c * GW, GW)
            own[m, :, part] = own[m, :, part] + rlow[m, :, part].astype(f32) + rup[m, :, part].astype(f32)
            cp = pltpu.make_async_copy(own.at[m, :, part], gl.at[m, :, part], outsm.at[m * GC + c])
            cp.start()
            outs.append(cp)

    xcp = []
    for j in range(NJ):
        for k in range(ENS - 1):
            ycp[j * (ENS - 1) + k].wait_recv()
        NG = RJ // 32
        half = pl.ds(j * NG, NG)
        v = ghk[half, :, cols(e, QC)]
        for k in range(ENS - 1):
            v = v + yr[k, half].astype(f32)
        zz = pl.ds(j * ZJ, ZJ)
        xk[zz] = v.reshape(ZJ, NX, 16, QC)
        xs[zz] = v.reshape(ZJ, NX, 16, QC).astype(bf16)
        for k in range(1, NX):
            cp = remote(
                xs.at[zz, (x + k) % NX], xr.at[k - 1, zz], xsm.at[k - 1, j], xrm.at[k - 1, j], xpeer[k - 1]
            )
            cp.start()
            xcp.append(cp)

    for cp in gx:
        cp.wait_recv()
    v = gzk[x]
    for k in range(NX - 1):
        v = v + gxr[k].astype(f32)
    gyv[...] = v
    gy = []
    for k in range(1, ENS):
        cp = remote(gyv, gyr.at[k - 1], gysm.at[k - 1], gyrm.at[k - 1], ypeer[k - 1])
        cp.start()
        gy.append(cp)

    for j in range(NJ):
        for k in range(NX - 1):
            xcp[j * (NX - 1) + k].wait_recv()
        zz = pl.ds(j * ZJ, ZJ)
        v = xk[zz, x]
        for k in range(NX - 1):
            v = v + xr[k, zz].astype(f32)
        xk[zz, x] = v
    zcp = []
    for k in range(1, NZ):
        cp = remote(xk.at[(z + k) % NZ, x], zr.at[k - 1], zsm.at[k - 1], zrm.at[k - 1], zpeer[k - 1])
        cp.start()
        zcp.append(cp)
    for cp in zcp:
        cp.wait_recv()
    v = xk[z, x]
    for k in range(NZ - 1):
        v = v + zr[k]
    ghv[:, cols(e, QC)] = v
    last = []
    for k in range(1, ENS):
        mine = ghv.at[:, cols(e, QC)]
        cp = remote(mine, mine, gsm.at[k], grm.at[k], ypeer[k - 1])
        cp.start()
    for cp in gy:
        cp.wait_recv()
    v = gyv[...]
    for k in range(ENS - 1):
        v = v + gyr[k]
    go[...] = v[:, :V]
    for k in range(1, ENS):
        src = (e + ENS - k) % ENS
        theirs = ghv.at[:, cols(src, QC)]
        pltpu.make_async_remote_copy(
            src_ref=theirs, dst_ref=theirs, send_sem=gsm.at[k], recv_sem=grm.at[k],
            device_id=ypeer[k - 1], device_id_type=MESH,
        ).wait_recv()
    gh[...] = ghv[...]
    for cp in outs:
        cp.wait()
    for cp in sends:
        cp.wait_send()


def shards(latents, edge_index, edge_weight, truth, w_hidden, output_weight):
    members = latents.shape[0] * lax.axis_size("ens")
    cells = truth.shape[1] * lax.axis_size("space")
    scale = 1.0 / math.sqrt(cells * members)
    any_ = pl.BlockSpec(memory_space=pl.ANY)
    vm = pl.BlockSpec(memory_space=pltpu.VMEM)
    dma = pltpu.SemaphoreType.DMA
    R2 = H // 32
    QC = H // ENS
    scratch = [
        pltpu.VMEM((2, 3 * NB, H), bf16),
        pltpu.VMEM((3 * NB, G), bf16),
        pltpu.VMEM((G, 3 * NB), bf16),
        pltpu.VMEM((H, H), bf16),
        pltpu.VMEM((H, H), bf16),
        pltpu.VMEM((V, H), bf16),
        pltpu.VMEM((VP, H), bf16),
        pltpu.VMEM((H, VP), bf16),
        pltpu.VMEM((4, G), jnp.int32),
        pltpu.VMEM((4, G), f32),
        pltpu.VMEM((V, QG), f32),
        pltpu.VMEM((VP, QG), f32),
        pltpu.VMEM((QG, VP), f32),
        pltpu.VMEM((G, FW), bf16),
        pltpu.VMEM((H, 2 * G), bf16),
        pltpu.VMEM((2, G, H), f32),
        pltpu.VMEM((2 * G, H), bf16),
        pltpu.VMEM((ENS - 1, 2, QG, VP), f32),
        pltpu.VMEM((ENS, 2, QG, VP), f32),
        pltpu.VMEM((ENS, 2, QG, VP), bf16),
        pltpu.VMEM((2, G, VP), bf16),
        pltpu.VMEM((VP, 2 * G), bf16),
        pltpu.VMEM((2 * G, H), bf16),
        pltpu.VMEM((G, 256), bf16),
        pltpu.VMEM((2, NB, H), bf16),
        pltpu.VMEM((2, NB, H), bf16),
        pltpu.VMEM((2, NB, H), bf16),
        pltpu.VMEM((2, NB, H), bf16),
        pltpu.VMEM((2, NB, H), f32),
        pltpu.VMEM((R2, 16, H), f32),
        pltpu.VMEM((R2, 16, H), bf16),
        pltpu.VMEM((R2, 16, H), bf16),
        pltpu.VMEM((8, 128), f32),
        pltpu.VMEM((R2, 16, H), bf16),
        pltpu.VMEM((ENS - 1, R2, 16, QC), bf16),
        pltpu.VMEM((NZ, NX, 16, QC), f32),
        pltpu.VMEM((NZ, NX, 16, QC), bf16),
        pltpu.VMEM((NX - 1, NZ, 16, QC), bf16),
        pltpu.VMEM((NZ - 1, 16, QC), f32),
        pltpu.VMEM((16, H), f32),
        pltpu.VMEM((R2, 16, VP), f32),
        pltpu.VMEM((R2, 16, VP), bf16),
        pltpu.VMEM((R2, 16, VP), bf16),
        pltpu.VMEM((NX, 16, VP), f32),
        pltpu.VMEM((R2, 16, VP), bf16),
        pltpu.VMEM((NZ - 1, NX, 16, VP), bf16),
        pltpu.VMEM((NX, 16, VP), bf16),
        pltpu.VMEM((NX - 1, 16, VP), bf16),
        pltpu.VMEM((16, VP), f32),
        pltpu.VMEM((ENS - 1, 16, VP), f32),
        dma((6,)),
        dma((2, 2 * FC)), dma((2, 2 * FC)),
        dma((ENS - 1, 2)), dma((ENS - 1, 2)),
        dma((ENS - 1,)), dma((ENS - 1,)),
        dma((2, 2 * GC)), dma((2, 2 * GC)),
        dma((NJ,)), dma((NJ,)),
        dma((ENS - 1, NJ)), dma((ENS - 1, NJ)),
        dma((NX - 1, NJ)), dma((NX - 1, NJ)),
        dma((NZ - 1,)), dma((NZ - 1,)),
        dma((ENS,)), dma((ENS,)),
        dma((NZ - 1,)), dma((NZ - 1,)),
        dma((NX - 1,)), dma((NX - 1,)),
        dma((ENS - 1,)), dma((ENS - 1,)),
        dma((2 * GC,)),
    ]
    return pl.pallas_call(
        functools.partial(kernel, scale),
        out_shape=(
            jax.ShapeDtypeStruct((2, NB, H), f32),
            jax.ShapeDtypeStruct((16, H), f32),
            jax.ShapeDtypeStruct((16, V), f32),
        ),
        in_specs=[any_] * 6,
        out_specs=(any_, vm, vm),
        scratch_shapes=scratch,
        compiler_params=pltpu.CompilerParams(
            collective_id=0, has_side_effects=True, vmem_limit_bytes=56 << 20
        ),
        name="decoder",
    )(latents, edge_index.T, edge_weight.T, truth, w_hidden, output_weight.T)


def solution(mesh):
    placed = (
        P("ens", "space", None),
        P("space", None),
        P("space", None),
        P(None, "space"),
        P(),
        P(),
    )
    return jax.shard_map(
        shards,
        mesh=mesh,
        in_specs=placed,
        out_specs=(P("ens", "space", None), P("space", None), P("space", None)),
        check_vma=False,
    )
```

time: 467 us -> 83.2 us (0.18)
  waiting for transfers between devices: 376 us -> 0 us
  Pallas kernels: 0 us -> 78 us
  matrix products: 29.8 us -> 0 us
  between operations: 14.6 us -> 0.66 us
  local copies, waits for them, and re-layouts: 18 us -> 4.43 us
  blocking collectives: 11.1 us -> 0 us
  starting transfers between devices: 8.97 us -> 0 us
  other arithmetic: 7.91 us -> 0 us
    unnamed x5 -> x0, waiting for transfers between devices: 156 us -> none
    reduce_scatter x1 -> x0, waiting for transfers between devices: 133 us -> none  [shards(): lax.psum_scatter(summed[0], 'space', scatter_dimension=0, tiled=True)]
    pallas_call x0 -> x1, Pallas kernels: none -> 78 us  [shards(): pl.pallas_call(functools.partial(kernel, scale), out_shape=(jax.ShapeDtyp...]
    psum x1 -> x0, waiting for transfers between devices: 40.6 us -> none  [shards(): summed = lax.psum((hidden_part, out_part), 'ens')]
    all_gather x1 -> x0, waiting for transfers between devices: 35.2 us -> none  [shards(): lax.all_gather(member_prediction, 'ens', axis=0, tiled=True)]
    dot_general x7 -> x0, matrix products: 29.8 us -> none  [the longest x1 8.26 us: shards(): jnp.einsum('gn,mgh->mnh', adjacency, daggregate, preferred_element_type=j...]
    ppermute x4 -> x0, waiting for transfers between devices: 12 us -> none  [the longest x1 7.49 us: extended(): lax.ppermute(head, axis, [((i + 1) % count, i) for i in range(ends)])]
    psum x1 -> x0, blocking collectives: 11.1 us -> none  [shards(): summed = lax.psum((hidden_part, out_part), 'ens')]
  transfers between devices with their start and end apart: 8 -> 0, of which waited for: 6 -> 0; matrix products, arithmetic and copies ran while one was open for 7% -> 0% of each run, Pallas kernels for 0% -> 0%
where the time goes in v1:
time: 83.2 us; the launch traced here: 83.1 us
  Pallas kernels  78 us (94%)
  local copies, waits for them, and re-layouts  4.43 us (5%)
    pallas_call x1, Pallas kernels, shards(): pl.pallas_call(functools.partial(kernel, scale), out_shape=(jax.ShapeDtyp...  78 us
    unnamed x7, local copies, waits for them, and re-layouts  4.43 us

profile of v1, /device:TPU:2, one launch (start us, length us, event | category | flops | bytes accessed | tf_op | source)
XLA Modules:
  0.0 83.1 jit_solution(4280114642202751321)
XLA Ops:
  0.6 78.0 %decoder.1 = (f32[2,256,1024]{2,1,0:T(8,128)}, f32[16,1024]{1,0:T(8,128)}, f32[16,100]{1,0:T(8,128)}) custom-call(bf16[2,256,1024]{2,1,0:T(8,128)(2,1)} %lat.1, s32[4,512]{1,0:T(4,128)} %bitcast.4, f32[4,512]{1,0:T(4,128)} %bitcast.5, f32[100,512]{1,0:T(8,128)} %truth.1, bf16[1024,1024]{1,0:T(8,128)(2,1)} %w.1, bf16[100,1024]{1,0:T(8,128)(2,1)} %bitcast.3), custom_call_target="tpu_custom_call" | custom-call | tf_op jit(solution)/shard_map/decoder/pallas_call | solution.py:475
  78.7 0.0 copy-start
  78.7 0.0 copy-start.1
  78.7 3.2 %copy.12 = f32[2,256,1024]{2,1,0:T(8,128)} copy(f32[2,256,1024]{2,1,0:T(8,128)} %get-tuple-element.6) | data formatting | bytes 4194304
  81.9 0.0 copy-done
  81.9 0.6 copy.13
  82.5 0.0 copy-done.1
  82.5 0.6 copy.14
Async XLA Ops:
  78.7 3.2 %copy-start = (f32[16,1024]{1,0:T(8,128)S(1)}, f32[16,1024]{1,0:T(8,128)}, u32[]{:S(2)}) copy-start(f32[16,1024]{1,0:T(8,128)} %get-tuple-element.7) | copy-start | bytes 196612
  78.7 3.8 %copy-start.1 = (f32[16,100]{1,0:T(8,128)S(1)}, f32[16,100]{1,0:T(8,128)}, u32[]{:S(2)}) copy-start(f32[16,100]{1,0:T(8,128)} %get-tuple-element.8) | copy-start | bytes 19204

commit v2 on v1

v2 whole, which is shorter than its diff:
```python
import functools
import math

import jax
import jax.numpy as jnp
from jax import lax
from jax.experimental import pallas as pl
from jax.experimental.pallas import tpu as pltpu
from jax.sharding import PartitionSpec as P

MESH = pl.DeviceIdType.MESH
f32 = jnp.float32
bf16 = jnp.bfloat16
smoothing = 0.05

H = 1024
V = 100
VP = 128
NB = 256
G = 512
ENS = 4
NZ, NX = 8, 4
SPACE = NZ * NX * 2
QG = G // ENS
QC = H // ENS
VS = 104
VM = 112
NJ = 2
LAG = 1
ZJ = NZ // NJ
PIECES = ((0, 0, 512), (0, 512, 512), (1, 0, 512), (1, 512, 256), (1, 768, 256))
AHEAD = 3
VLIM = 56
CUTS = 8
GPIECES = ((0, 0, 512), (0, 512, 512), (1, 0, 512), (1, 512, 512))


def mm(a, b):
    return jnp.dot(a, b, preferred_element_type=f32)


def cols(i, width):
    return pl.ds(pl.multiple_of(i * width, width), width)


def nt(a, b):
    return lax.dot_general(a, b, (((1,), (1,)), ((), ())), preferred_element_type=f32)


def tn(a, b):
    return lax.dot_general(a, b, (((0,), (0,)), ((), ())), preferred_element_type=f32)


def kernel(
    scale,
    lat, ei, ew, truth, w, wot,
    gl, gh, go,
    xw, at, a, wv, wotr, wotv, eiv, ewv, trr, trv,
    agg, pre, act, fcs, fcr, dfs, dfr, dpre, daggc,
    low, up, rlow, rup, own,
    ghk, ghs, ghr, ys, yr, xk, xs, xr, zs, zr, ghv,
    gok, gos, gor, gzk, gzs, gzr, gxs, gxr, gyv, gyr,
    ld, fs, fr, es, er, bs, br, hs, hr, cs, cr, ysm, yrm, xsm, xrm, zsm, zrm, gsm, grm,
    gzsm, gzrm, gxsm, gxrm, gysm, gyrm, outsm,
):
    e = lax.axis_index("ens")
    s = lax.axis_index("space")
    z = s // 8
    x = (s // 2) % NX
    core = s % 2
    right = (e, (s + 1) % SPACE)
    left = (e, (s + SPACE - 1) % SPACE)
    mate = (e, z * 8 + x * 2 + (1 - core))
    ypeer = [((e + k) % ENS, s) for k in range(1, ENS)]
    xpeer = [(e, z * 8 + ((x + k) % NX) * 2 + core) for k in range(1, NX)]
    zpeer = [(e, ((z + k) % NZ) * 8 + x * 2 + core) for k in range(1, NZ)]

    def remote(src, dst, ssem, rsem, to):
        cp = pltpu.make_async_remote_copy(
            src_ref=src, dst_ref=dst, send_sem=ssem, recv_sem=rsem, device_id=to, device_id_type=MESH
        )
        sends.append(cp)
        return cp

    sends = []
    barrier = pltpu.get_barrier_semaphore()
    everyone = [left, right, mate] + ypeer + xpeer + zpeer
    for to in everyone:
        pl.semaphore_signal(barrier, inc=1, device_id=to, device_id_type=MESH)

    loads = [
        pltpu.make_async_copy(ei, eiv, ld.at[0]),
        pltpu.make_async_copy(ew, ewv, ld.at[1]),
        pltpu.make_async_copy(lat, xw.at[:, pl.ds(NB, NB)], ld.at[2]),
        pltpu.make_async_copy(w, wv, ld.at[3]),
        pltpu.make_async_copy(wot, wotr, ld.at[4]),
        pltpu.make_async_copy(truth.at[:, cols(e, QG)], trr, ld.at[5]),
    ]
    for cp in loads:
        cp.start()
    pl.semaphore_wait(barrier, len(everyone))

    halo = {}

    def send_halo(i):
        m, first, width = PIECES[i]
        part = lat.at[m, :, pl.ds(first, width)]
        up_cp = remote(part, xw.at[m, pl.ds(0, NB), pl.ds(first, width)], fs.at[0, i], fr.at[0, i], right)
        dn_cp = remote(part, xw.at[m, pl.ds(2 * NB, NB), pl.ds(first, width)], fs.at[1, i], fr.at[1, i], left)
        up_cp.start()
        dn_cp.start()
        halo[i] = (up_cp, dn_cp)

    for i in range(AHEAD):
        send_halo(i)

    loads[0].wait()
    loads[1].wait()
    wr = ewv[...].astype(bf16).astype(f32)

    @pl.loop(0, 3 * NB // 128)
    def _(b):
        row = lax.broadcasted_iota(jnp.int32, (128, G), 0) + b * 128
        t = jnp.zeros((128, G), f32)
        for k in range(4):
            t = jnp.where(row == eiv[pl.ds(k, 1), :], wr[k : k + 1, :], t)
        at[cols(b, 128), :] = t.astype(bf16)
        a[:, cols(b, 128)] = t.T.astype(bf16)

    for cp in loads[2:]:
        cp.wait()
    wotv[...] = jnp.concatenate([wotr[...], jnp.zeros((VP - V, H), bf16)], axis=0)
    trv[...] = jnp.concatenate([trr[...], jnp.zeros((VM - V, QG), f32)], axis=0)
    for k in range(ENS):
        for m in range(2):
            fcr[k, m, pl.ds(VS, VM - VS), :] = jnp.zeros((VM - VS, QG), f32)
    for m in range(2):
        dfr[m, pl.ds(VM, VP - VM), :] = jnp.zeros((VP - VM, G), bf16)

    def slope(m):
        @pl.loop(0, H // 256)
        def _(t):
            v = pre[m, :, cols(t, 256)]
            sg = jax.nn.sigmoid(v)
            pre[m, :, cols(t, 256)] = sg * (1.0 + v * (1.0 - sg))

    for i, (m, first, width) in enumerate(PIECES):
        for cp in halo[i]:
            cp.wait_recv()
        if i + AHEAD < len(PIECES):
            send_halo(i + AHEAD)
        part = pl.ds(first, width)
        agg[pl.ds(m * G, G), part] = mm(a[...], xw[m, :, part]).astype(bf16)
        v = mm(agg[pl.ds(m * G, G), part], wv[part, :])
        if first > 0:
            v = v + pre[m]
        pre[m] = v
        if first + width < H:
            continue
        for k in range(ENS):
            r = (e + 1 + k) % ENS
            rows = cols(r, QG)
            arows = pl.ds(pl.multiple_of(m * G + r * QG, QG), QG)
            v = pre[m, rows, :]
            act[arows, :] = (v * jax.nn.sigmoid(v)).astype(bf16)
            fc = nt(wotv[pl.ds(0, VM), :], act[arows, :])
            if k < ENS - 1:
                fcs[k, m] = fc[:VS]
                remote(
                    fcs.at[k, m], fcr.at[k, m, pl.ds(0, VS)], es.at[k, m], er.at[k, m], ypeer[k]
                ).start()
            else:
                fcr[k, m, pl.ds(0, VS), :] = fc[:VS]
        slope(m)

    for m in range(2):
        for k in range(ENS - 1):
            pltpu.make_async_remote_copy(
                src_ref=fcs.at[k, m], dst_ref=fcr.at[k, m, pl.ds(0, VS)], send_sem=es.at[k, m],
                recv_sem=er.at[k, m], device_id=ypeer[k], device_id_type=MESH,
            ).wait_recv()

    members = 2 * ENS

    @pl.loop(0, VM // 16)
    def _(b):
        rows = cols(b, 16)
        f = [fcr[i // 2, i % 2, rows, :] for i in range(members)]
        tr = trv[rows, :]
        total = [jnp.zeros((16, QG), f32) for _ in range(members)]
        for i in range(members):
            for j in range(i + 1, members):
                d = f[i] - f[j]
                q = d * lax.rsqrt(d * d + smoothing * smoothing)
                total[i] = total[i] + q
                total[j] = total[j] - q
        for i in range(members):
            d = f[i] - tr
            q = d * lax.rsqrt(d * d + smoothing * smoothing)
            dfs[i // 2, i % 2, rows, :] = (
                scale * (q * (1.0 / members) - total[i] * (1.0 / (members * (members - 1))))
            ).astype(bf16)

    for k in range(ENS - 1):
        back = ((e + ENS - 1 - k) % ENS, s)
        remote(dfs.at[k], dfr.at[:, pl.ds(0, VM), cols(e, QG)], bs.at[k], br.at[k], back).start()
    dfr[:, pl.ds(0, VM), cols(e, QG)] = dfs[ENS - 1]
    for k in range(ENS - 1):
        src = (e + 1 + k) % ENS
        pltpu.make_async_remote_copy(
            src_ref=dfs.at[k], dst_ref=dfr.at[:, pl.ds(0, VM), cols(src, QG)], send_sem=bs.at[k],
            recv_sem=br.at[k], device_id=((e + ENS - 1 - k) % ENS, s), device_id_type=MESH,
        ).wait_recv()

    for m in range(2):
        dpre[pl.ds(m * G, G), :] = (tn(dfr[m], wotv[...]) * pre[m]).astype(bf16)

    RJ = H // NJ
    NG = RJ // 32
    gcore = []
    ycp = []

    def send_y(j):
        gcore[j].wait_recv()
        groups = pl.ds(j * NG, NG)
        v = ghk[groups] + ghr[groups].astype(f32)
        ghk[groups] = v
        for k in range(ENS):
            ys[k, groups] = v[:, :, k * QC : (k + 1) * QC].astype(bf16)
        for k in range(1, ENS):
            cp = remote(
                ys.at[(e + k) % ENS, groups], yr.at[k - 1, groups], ysm.at[k - 1, j],
                yrm.at[k - 1, j], ypeer[k - 1],
            )
            cp.start()
            ycp.append(cp)

    grads = []

    def node_grads(i):
        m, first, width = GPIECES[i]
        part = pl.ds(first, width)
        daggc[:, pl.ds(0, width)] = nt(dpre[pl.ds(m * G, G), :], wv[part, :]).astype(bf16)
        v = mm(at[...], daggc[:, pl.ds(0, width)])
        low[i] = v[:NB].astype(bf16)
        up[i] = v[2 * NB :].astype(bf16)
        own[m, :, part] = v[NB : 2 * NB]
        one = remote(low.at[i], rlow.at[i], hs.at[0, i], hr.at[0, i], left)
        two = remote(up.at[i], rup.at[i], hs.at[1, i], hr.at[1, i], right)
        one.start()
        two.start()
        grads.append((one, two))

    node_grads(0)
    node_grads(1)
    for j in range(NJ):
        v = tn(agg[:, pl.ds(j * RJ, RJ)], dpre[...]).reshape(NG, 2, 16, H)
        groups = pl.ds(j * NG, NG)
        ghk[groups] = jnp.where(core == 0, v[:, 0], v[:, 1])
        ghs[groups] = jnp.where(core == 0, v[:, 1], v[:, 0]).astype(bf16)
        cp = remote(ghs.at[groups], ghr.at[groups], cs.at[j], cr.at[j], mate)
        cp.start()
        gcore.append(cp)
        if j >= LAG:
            send_y(j - LAG)
    node_grads(2)
    for j in range(NJ - LAG, NJ):
        send_y(j)
    for i in range(3, len(GPIECES)):
        node_grads(i)

    v = mm(dfr[0], act[pl.ds(0, G), :]) + mm(dfr[1], act[pl.ds(G, G), :])
    v = v.T.reshape(H // 32, 2, 16, VP)
    gok[...] = jnp.where(core == 0, v[:, 0], v[:, 1])
    gos[...] = jnp.where(core == 0, v[:, 1], v[:, 0]).astype(bf16)
    gcp = remote(gos, gor, gsm.at[0], grm.at[0], mate)
    gcp.start()
    gcp.wait_recv()
    gzs[...] = (gok[...] + gor[...].astype(f32)).astype(bf16)
    gz = []
    for k in range(1, NZ):
        cp = remote(gzs.at[cols((z + k) % NZ, NX)], gzr.at[k - 1], gzsm.at[k - 1], gzrm.at[k - 1], zpeer[k - 1])
        cp.start()
        gz.append(cp)
    gzk[...] = gok[cols(z, NX)] + gor[cols(z, NX)].astype(f32)

    for cp in gz:
        cp.wait_recv()
    v = gzk[...]
    for k in range(NZ - 1):
        v = v + gzr[k].astype(f32)
    gzk[...] = v
    gxs[...] = v.astype(bf16)
    gx = []
    for k in range(1, NX):
        cp = remote(gxs.at[(x + k) % NX], gxr.at[k - 1], gxsm.at[k - 1], gxrm.at[k - 1], xpeer[k - 1])
        cp.start()
        gx.append(cp)

    xcp = []

    def send_x(j):
        for k in range(ENS - 1):
            ycp[j * (ENS - 1) + k].wait_recv()
        groups = pl.ds(j * NG, NG)
        v = ghk[groups, :, cols(e, QC)]
        for k in range(ENS - 1):
            v = v + yr[k, groups].astype(f32)
        zz = pl.ds(j * ZJ, ZJ)
        xk[zz] = v.reshape(ZJ, NX, 16, QC)
        for k in range(NX):
            xs[k, zz] = xk[zz, k].astype(bf16)
        for k in range(1, NX):
            cp = remote(
                xs.at[(x + k) % NX, zz], xr.at[k - 1, zz], xsm.at[k - 1, j], xrm.at[k - 1, j], xpeer[k - 1]
            )
            cp.start()
            xcp.append(cp)

    def add_x(j):
        for k in range(NX - 1):
            xcp[j * (NX - 1) + k].wait_recv()
        zz = pl.ds(j * ZJ, ZJ)
        v = xk[zz, x]
        for k in range(NX - 1):
            v = v + xr[k, zz].astype(f32)
        xk[zz, x] = v
        zs[zz] = v.astype(bf16)

    outs = []

    def finish(i):
        m, first, width = GPIECES[i]
        for cp in grads[i]:
            cp.wait_recv()
        part = pl.ds(first, width)
        own[m, :, part] = own[m, :, part] + rlow[i].astype(f32) + rup[i].astype(f32)
        cp = pltpu.make_async_copy(own.at[m, :, part], gl.at[m, :, part], outsm.at[i])
        cp.start()
        outs.append(cp)

    left_over = list(range(len(GPIECES)))
    for j in range(NJ):
        send_x(j)
        if j >= 1:
            add_x(j - 1)
        if j < NJ - 1:
            finish(left_over.pop(0))

    for cp in gx:
        cp.wait_recv()
    v = gzk[x]
    for k in range(NX - 1):
        v = v + gxr[k].astype(f32)
    gyv[...] = v
    gy = []
    for k in range(1, ENS):
        cp = remote(gyv, gyr.at[k - 1], gysm.at[k - 1], gyrm.at[k - 1], ypeer[k - 1])
        cp.start()
        gy.append(cp)

    add_x(NJ - 1)
    zcp = []
    for k in range(1, NZ):
        cp = remote(zs.at[(z + k) % NZ], zr.at[k - 1], zsm.at[k - 1], zrm.at[k - 1], zpeer[k - 1])
        cp.start()
        zcp.append(cp)
    for i in left_over:
        finish(i)
    for cp in gy:
        cp.wait_recv()
    v = gyv[...]
    for k in range(ENS - 1):
        v = v + gyr[k]
    go[...] = v[:, :V]
    for cp in zcp:
        cp.wait_recv()
    v = xk[z, x]
    for k in range(NZ - 1):
        v = v + zr[k].astype(f32)
    ghv[:, cols(e, QC)] = v
    for k in range(1, ENS):
        mine = ghv.at[:, cols(e, QC)]
        remote(mine, mine, gsm.at[k], grm.at[k], ypeer[k - 1]).start()
    for k in range(1, ENS):
        src = (e + ENS - k) % ENS
        theirs = ghv.at[:, cols(src, QC)]
        pltpu.make_async_remote_copy(
            src_ref=theirs, dst_ref=theirs, send_sem=gsm.at[k], recv_sem=grm.at[k],
            device_id=ypeer[k - 1], device_id_type=MESH,
        ).wait_recv()
    gh[...] = ghv[...]
    for cp in outs:
        cp.wait()
    for cp in sends:
        cp.wait_send()


def hand_over(a, b, c, oa, ob, oc, va, vb, vc, isem, osem):
    rows = a.shape[1] // CUTS * 2
    places = [(i % 2, pl.ds(i // 2 * rows, rows)) for i in range(CUTS)]
    moves = [(a.at[p], va.at[p], oa.at[p]) for p in places] + [(b, vb, ob), (c, vc, oc)]
    ins = [pltpu.make_async_copy(src, mid, isem.at[i]) for i, (src, mid, _) in enumerate(moves)]
    outs = [pltpu.make_async_copy(mid, dst, osem.at[i]) for i, (_, mid, dst) in enumerate(moves)]
    for cp in ins:
        cp.start()
    for one, two in zip(ins, outs):
        one.wait()
        two.start()
    for cp in outs:
        cp.wait()


def shards(latents, edge_index, edge_weight, truth, w_hidden, output_weight):
    members = latents.shape[0] * lax.axis_size("ens")
    cells = truth.shape[1] * lax.axis_size("space")
    scale = 1.0 / math.sqrt(cells * members)
    any_ = pl.BlockSpec(memory_space=pl.ANY)
    vm = pl.BlockSpec(memory_space=pltpu.VMEM)
    dma = pltpu.SemaphoreType.DMA
    R2 = H // 32
    scratch = [
        pltpu.VMEM((2, 3 * NB, H), bf16),
        pltpu.VMEM((3 * NB, G), bf16),
        pltpu.VMEM((G, 3 * NB), bf16),
        pltpu.VMEM((H, H), bf16),
        pltpu.VMEM((V, H), bf16),
        pltpu.VMEM((VP, H), bf16),
        pltpu.VMEM((4, G), jnp.int32),
        pltpu.VMEM((4, G), f32),
        pltpu.VMEM((V, QG), f32),
        pltpu.VMEM((VM, QG), f32),
        pltpu.VMEM((2 * G, H), bf16),
        pltpu.VMEM((2, G, H), f32),
        pltpu.VMEM((2 * G, H), bf16),
        pltpu.VMEM((ENS - 1, 2, VS, QG), f32),
        pltpu.VMEM((ENS, 2, VM, QG), f32),
        pltpu.VMEM((ENS, 2, VM, QG), bf16),
        pltpu.VMEM((2, VP, G), bf16),
        pltpu.VMEM((2 * G, H), bf16),
        pltpu.VMEM((G, 512), bf16),
        pltpu.VMEM((len(GPIECES), NB, 512), bf16),
        pltpu.VMEM((len(GPIECES), NB, 512), bf16),
        pltpu.VMEM((len(GPIECES), NB, 512), bf16),
        pltpu.VMEM((len(GPIECES), NB, 512), bf16),
        pltpu.VMEM((2, NB, H), f32),
        pltpu.VMEM((R2, 16, H), f32),
        pltpu.VMEM((R2, 16, H), bf16),
        pltpu.VMEM((R2, 16, H), bf16),
        pltpu.VMEM((ENS, R2, 16, QC), bf16),
        pltpu.VMEM((ENS - 1, R2, 16, QC), bf16),
        pltpu.VMEM((NZ, NX, 16, QC), f32),
        pltpu.VMEM((NX, NZ, 16, QC), bf16),
        pltpu.VMEM((NX - 1, NZ, 16, QC), bf16),
        pltpu.VMEM((NZ, 16, QC), bf16),
        pltpu.VMEM((NZ - 1, 16, QC), bf16),
        pltpu.VMEM((16, H), f32),
        pltpu.VMEM((R2, 16, VP), f32),
        pltpu.VMEM((R2, 16, VP), bf16),
        pltpu.VMEM((R2, 16, VP), bf16),
        pltpu.VMEM((NX, 16, VP), f32),
        pltpu.VMEM((R2, 16, VP), bf16),
        pltpu.VMEM((NZ - 1, NX, 16, VP), bf16),
        pltpu.VMEM((NX, 16, VP), bf16),
        pltpu.VMEM((NX - 1, 16, VP), bf16),
        pltpu.VMEM((16, VP), f32),
        pltpu.VMEM((ENS - 1, 16, VP), f32),
        dma((6,)),
        dma((2, len(PIECES))), dma((2, len(PIECES))),
        dma((ENS - 1, 2)), dma((ENS - 1, 2)),
        dma((ENS - 1,)), dma((ENS - 1,)),
        dma((2, len(GPIECES))), dma((2, len(GPIECES))),
        dma((NJ,)), dma((NJ,)),
        dma((ENS - 1, NJ)), dma((ENS - 1, NJ)),
        dma((NX - 1, NJ)), dma((NX - 1, NJ)),
        dma((NZ - 1,)), dma((NZ - 1,)),
        dma((ENS,)), dma((ENS,)),
        dma((NZ - 1,)), dma((NZ - 1,)),
        dma((NX - 1,)), dma((NX - 1,)),
        dma((ENS - 1,)), dma((ENS - 1,)),
        dma((len(GPIECES),)),
    ]
    held = pl.pallas_call(
        functools.partial(kernel, scale),
        out_shape=(
            jax.ShapeDtypeStruct((2, NB, H), f32),
            jax.ShapeDtypeStruct((16, H), f32),
            jax.ShapeDtypeStruct((16, V), f32),
        ),
        in_specs=[any_] * 6,
        out_specs=(any_, vm, vm),
        scratch_shapes=scratch,
        compiler_params=pltpu.CompilerParams(
            collective_id=0, has_side_effects=True, vmem_limit_bytes=VLIM << 20
        ),
        name="decoder",
    )(latents, edge_index.T, edge_weight.T, truth, w_hidden, output_weight.T)
    return pl.pallas_call(
        hand_over,
        out_shape=[jax.ShapeDtypeStruct(v.shape, v.dtype) for v in held],
        in_specs=[any_] * 3,
        out_specs=[any_] * 3,
        scratch_shapes=[pltpu.VMEM(v.shape, v.dtype) for v in held] + [dma((CUTS + 2,)), dma((CUTS + 2,))],
        name="hand_over",
    )(*held)


def solution(mesh):
    placed = (
        P("ens", "space", None),
        P("space", None),
        P("space", None),
        P(None, "space"),
        P(),
        P(),
    )
    return jax.shard_map(
        shards,
        mesh=mesh,
        in_specs=placed,
        out_specs=(P("ens", "space", None), P("space", None), P("space", None)),
        check_vma=False,
    )
```

time: 83.2 us -> 72 us (0.87)
  Pallas kernels: 78 us -> 71 us
  local copies, waits for them, and re-layouts: 4.43 us -> 0 us
    pallas_call x1, Pallas kernels: 78 us -> 68.5 us  [shards(): pl.pallas_call(functools.partial(kernel, scale), out_shape=(jax.ShapeDtyp...]
    unnamed x7 -> x0, local copies, waits for them, and re-layouts: 4.43 us -> none
    pallas_call x0 -> x1, Pallas kernels: none -> 2.45 us  [shards(): pl.pallas_call(hand_over, out_shape=[jax.ShapeDtypeStruct(v.shape, v.dtyp...]
where the time goes in v2:
time: 72 us; the launch traced here: 71.8 us
  Pallas kernels  71 us (99%)
  between operations  0.8 us (1%)
    pallas_call x1, Pallas kernels, shards(): pl.pallas_call(functools.partial(kernel, scale), out_shape=(jax.ShapeDtyp...  68.5 us
    pallas_call x1, Pallas kernels, shards(): pl.pallas_call(hand_over, out_shape=[jax.ShapeDtypeStruct(v.shape, v.dtyp...  2.45 us

profile of v2, /device:TPU:2, one launch (start us, length us, event | category | flops | bytes accessed | tf_op | source)
XLA Modules:
  0.0 71.8 jit_solution(13167411508747980328)
XLA Ops:
  0.6 68.5 %decoder.1 = (f32[2,256,1024]{2,1,0:T(8,128)}, f32[16,1024]{1,0:T(8,128)}, f32[16,100]{1,0:T(8,128)}) custom-call(bf16[2,256,1024]{2,1,0:T(8,128)(2,1)} %lat.1, s32[4,512]{1,0:T(4,128)} %bitcast.4, f32[4,512]{1,0:T(4,128)} %bitcast.5, f32[100,512]{1,0:T(8,128)} %truth.1, bf16[1024,1024]{1,0:T(8,128)(2,1)} %w.1, bf16[100,1024]{1,0:T(8,128)(2,1)} %bitcast.3), custom_call_target="tpu_custom_call" | custom-call | tf_op jit(solution)/shard_map/decoder/pallas_call | solution.py:483
  69.2 2.4 %hand_over.1 = (f32[2,256,1024]{2,1,0:T(8,128)}, f32[16,1024]{1,0:T(8,128)}, f32[16,100]{1,0:T(8,128)}) custom-call(f32[2,256,1024]{2,1,0:T(8,128)} %get-tuple-element.6.a, f32[16,1024]{1,0:T(8,128)} %get-tuple-element.7.b, f32[16,100]{1,0:T(8,128)} %get-tuple-element.8.c), custom_call_target="tpu_custom_call" | custom-call | tf_op jit(solution)/shard_map/hand_over/pallas_call | solution.py:498

commit v3 on v2

--- a/solution.py
+++ b/solution.py
@@ -201,18 +201,21 @@
                 scale * (q * (1.0 / members) - total[i] * (1.0 / (members * (members - 1))))
             ).astype(bf16)
 
-    for k in range(ENS - 1):
-        back = ((e + ENS - 1 - k) % ENS, s)
-        remote(dfs.at[k], dfr.at[:, pl.ds(0, VM), cols(e, QG)], bs.at[k], br.at[k], back).start()
-    dfr[:, pl.ds(0, VM), cols(e, QG)] = dfs[ENS - 1]
-    for k in range(ENS - 1):
-        src = (e + 1 + k) % ENS
-        pltpu.make_async_remote_copy(
-            src_ref=dfs.at[k], dst_ref=dfr.at[:, pl.ds(0, VM), cols(src, QG)], send_sem=bs.at[k],
-            recv_sem=br.at[k], device_id=((e + ENS - 1 - k) % ENS, s), device_id_type=MESH,
-        ).wait_recv()
-
     for m in range(2):
+        for k in range(ENS - 1):
+            back = ((e + ENS - 1 - k) % ENS, s)
+            remote(
+                dfs.at[k, m], dfr.at[m, pl.ds(0, VM), cols(e, QG)], bs.at[k, m], br.at[k, m], back
+            ).start()
+        dfr[m, pl.ds(0, VM), cols(e, QG)] = dfs[ENS - 1, m]
+
+    def dpreact(m):
+        for k in range(ENS - 1):
+            src = (e + 1 + k) % ENS
+            pltpu.make_async_remote_copy(
+                src_ref=dfs.at[k, m], dst_ref=dfr.at[m, pl.ds(0, VM), cols(src, QG)], send_sem=bs.at[k, m],
+                recv_sem=br.at[k, m], device_id=((e + ENS - 1 - k) % ENS, s), device_id_type=MESH,
+            ).wait_recv()
         dpre[pl.ds(m * G, G), :] = (tn(dfr[m], wotv[...]) * pre[m]).astype(bf16)
 
     RJ = H // NJ
@@ -251,8 +254,10 @@
         two.start()
         grads.append((one, two))
 
+    dpreact(0)
     node_grads(0)
     node_grads(1)
+    dpreact(1)
     for j in range(NJ):
         v = tn(agg[:, pl.ds(j * RJ, RJ)], dpre[...]).reshape(NG, 2, 16, H)
         groups = pl.ds(j * NG, NG)
@@ -468,7 +473,7 @@
         dma((6,)),
         dma((2, len(PIECES))), dma((2, len(PIECES))),
         dma((ENS - 1, 2)), dma((ENS - 1, 2)),
-        dma((ENS - 1,)), dma((ENS - 1,)),
+        dma((ENS - 1, 2)), dma((ENS - 1, 2)),
         dma((2, len(GPIECES))), dma((2, len(GPIECES))),
         dma((NJ,)), dma((NJ,)),
         dma((ENS - 1, NJ)), dma((ENS - 1, NJ)),

time: 72 us -> 71.6 us (level)
  no operation moved by 1% of the time
where the time goes in v3:
time: 71.6 us; the launch traced here: 71.3 us
  Pallas kernels  70.5 us (98%)
  between operations  0.8 us (1%)
    pallas_call x1, Pallas kernels, shards(): pl.pallas_call(functools.partial(kernel, scale), out_shape=(jax.ShapeDtyp...  68.1 us
    pallas_call x1, Pallas kernels, shards(): pl.pallas_call(hand_over, out_shape=[jax.ShapeDtypeStruct(v.shape, v.dtyp...  2.45 us

profile of v3, /device:TPU:2, one launch (start us, length us, event | category | flops | bytes accessed | tf_op | source)
XLA Modules:
  0.0 71.3 jit_solution(1754535926263494)
XLA Ops:
  0.6 68.1 %decoder.1 = (f32[2,256,1024]{2,1,0:T(8,128)}, f32[16,1024]{1,0:T(8,128)}, f32[16,100]{1,0:T(8,128)}) custom-call(bf16[2,256,1024]{2,1,0:T(8,128)(2,1)} %lat.1, s32[4,512]{1,0:T(4,128)} %bitcast.4, f32[4,512]{1,0:T(4,128)} %bitcast.5, f32[100,512]{1,0:T(8,128)} %truth.1, bf16[1024,1024]{1,0:T(8,128)(2,1)} %w.1, bf16[100,1024]{1,0:T(8,128)(2,1)} %bitcast.3), custom_call_target="tpu_custom_call" | custom-call | tf_op jit(solution)/shard_map/decoder/pallas_call | solution.py:488
  68.7 2.4 %hand_over.1 = (f32[2,256,1024]{2,1,0:T(8,128)}, f32[16,1024]{1,0:T(8,128)}, f32[16,100]{1,0:T(8,128)}) custom-call(f32[2,256,1024]{2,1,0:T(8,128)} %get-tuple-element.6.a, f32[16,1024]{1,0:T(8,128)} %get-tuple-element.7.b, f32[16,100]{1,0:T(8,128)} %get-tuple-element.8.c), custom_call_target="tpu_custom_call" | custom-call | tf_op jit(solution)/shard_map/hand_over/pallas_call | solution.py:503
